TPU v7x, 32 devices: a whole 2x2x4 slice. The times are simulated.
32 devices in a mesh: expert: 4 (over y, x), hidden: 8 (over z, core).
Axes of the slice: x: 2, y: 2, z: 4, core: 2. Of those that a mesh axis runs over, the one named last changes fastest.
Arguments:
- tokens: bfloat16 [192, 6144], P(('expert', 'hidden')), may hold values from -6 to 6
- routes: int32 [192, 2], P(('expert', 'hidden')), may hold values from 0 to 3, all different within a row; in each aligned block of 6 rows (0 to 5, 6 to 11, ...) at most 4 rows name the same one
- gate_probs: float32 [192, 2], P(('expert', 'hidden')), may hold values from 0.1 to 1
- cotangent: bfloat16 [192, 6144], P(('expert', 'hidden')), may hold values from -6 to 6
- w_gate: bfloat16 [4, 6144, 8192], P('expert', None, 'hidden'), may hold values from -0.078125 to 0.078125
- w_up: bfloat16 [4, 6144, 8192], P('expert', None, 'hidden'), may hold values from -0.078125 to 0.078125
- w_down: bfloat16 [4, 8192, 6144], P('expert', 'hidden'), may hold values from -0.0625 to 0.0625
Outputs:
- layer_out: bfloat16 [192, 6144], P(('expert', 'hidden'))
- grad_tokens: bfloat16 [192, 6144], P(('expert', 'hidden'))
- grad_gate: bfloat16 [4, 6144, 8192], P('expert', None, 'hidden')
- grad_up: bfloat16 [4, 6144, 8192], P('expert', None, 'hidden')
- grad_down: bfloat16 [4, 8192, 6144], P('expert', 'hidden')
Inputs may be any that keep to these rules, and one draw needn't show every extreme that they name: `routes`: each row names two different experts. Within the tokens of one device (aligned blocks of 6 rows) no expert is named by more than 4 rows, a bound that some block reaches.
All inputs are finite; a program needn't handle non-finite values.
Results may differ from a plain program's by a relative error of at most 0.015.
Values may be sent and summed in bfloat16 or wider, within the bound.
A program may use at most 192 MiB of HBM per device.

v0:
```python
import jax
import jax.numpy as jnp
from jax import lax
from jax.sharding import PartitionSpec as P


def slot_table(route_ids, experts, capacity):
    flat_ids = route_ids.reshape(-1)
    hits = (flat_ids[:, None] == jnp.arange(experts, dtype=jnp.int32)[None, :]).astype(jnp.int32)
    before = jnp.cumsum(hits, axis=0) - hits
    ranks = jnp.sum(before * hits, axis=1)
    slot_ids = flat_ids * capacity + ranks
    table = (slot_ids[:, None] == jnp.arange(experts * capacity, dtype=jnp.int32)[None, :]).astype(
        jnp.float32
    )
    return table.reshape(route_ids.shape[0], 2, experts * capacity)


def on_device(tokens, routes, gate_probs, cotangent, w_gate, w_up, w_down):
    experts = lax.axis_size("expert")
    width = tokens.shape[1]
    capacity = (2 * tokens.shape[0] + experts - 1) // experts + 1
    table = slot_table(routes, experts, capacity)
    placed = jnp.sum(table, axis=1)
    weighted = jnp.sum(table * gate_probs[:, :, None], axis=1)
    send_in = jnp.dot(
        placed.T.astype(jnp.bfloat16), tokens, preferred_element_type=jnp.float32
    ).astype(jnp.bfloat16)
    send_grad = jnp.dot(
        weighted.T, cotangent.astype(jnp.float32), precision=lax.Precision.HIGHEST
    ).astype(jnp.bfloat16)
    send_in = send_in.reshape(experts, capacity, width)
    send_grad = send_grad.reshape(experts, capacity, width)
    grouped = (
        lax.all_gather(send_in[None], "hidden", axis=0, tiled=True),
        lax.all_gather(send_grad[None], "hidden", axis=0, tiled=True),
    )
    arrived = (
        lax.all_to_all(grouped[0], "expert", split_axis=1, concat_axis=1, tiled=True),
        lax.all_to_all(grouped[1], "expert", split_axis=1, concat_axis=1, tiled=True),
    )
    expert_rows = arrived[0].reshape(-1, width)
    grad_rows = arrived[1].reshape(-1, width)
    gate_w = w_gate[0]
    up_w = w_up[0]
    down_w = w_down[0]
    pre_gate = jnp.dot(expert_rows, gate_w, preferred_element_type=jnp.float32)
    pre_up = jnp.dot(expert_rows, up_w, preferred_element_type=jnp.float32)
    sig_gate = jax.nn.sigmoid(pre_gate)
    hidden = (pre_gate * sig_gate * pre_up).astype(jnp.bfloat16)
    summed_out = lax.psum_scatter(
        jnp.dot(hidden, down_w, preferred_element_type=jnp.float32).astype(jnp.bfloat16),
        "hidden",
        scatter_dimension=0,
        tiled=True,
    )
    expert_out = summed_out.reshape(experts, capacity, width)
    returned = lax.all_to_all(expert_out, "expert", split_axis=0, concat_axis=0, tiled=True)
    layer_out = jnp.dot(
        weighted, returned.reshape(-1, width).astype(jnp.float32), precision=lax.Precision.HIGHEST
    ).astype(jnp.bfloat16)
    grad_hidden = jnp.dot(grad_rows, down_w.T, preferred_element_type=jnp.float32)
    grad_pre_gate = (grad_hidden * pre_up * sig_gate * (1.0 + pre_gate * (1.0 - sig_gate))).astype(
        jnp.bfloat16
    )
    grad_pre_up = (grad_hidden * pre_gate * sig_gate).astype(jnp.bfloat16)
    grad_down = jnp.dot(hidden.T, grad_rows, preferred_element_type=jnp.float32).astype(
        jnp.bfloat16
    )
    grad_gate = jnp.dot(expert_rows.T, grad_pre_gate, preferred_element_type=jnp.float32).astype(
        jnp.bfloat16
    )
    grad_up = jnp.dot(expert_rows.T, grad_pre_up, preferred_element_type=jnp.float32).astype(
        jnp.bfloat16
    )
    first = jnp.dot(grad_pre_gate, gate_w.T, preferred_element_type=jnp.float32)
    summed_back = lax.psum_scatter(
        (first + jnp.dot(grad_pre_up, up_w.T, preferred_element_type=jnp.float32)).astype(
            jnp.bfloat16
        ),
        "hidden",
        scatter_dimension=0,
        tiled=True,
    )
    expert_back = summed_back.reshape(experts, capacity, width)
    returned_back = lax.all_to_all(expert_back, "expert", split_axis=0, concat_axis=0, tiled=True)
    grad_tokens = jnp.dot(
        placed,
        returned_back.reshape(-1, width).astype(jnp.float32),
        precision=lax.Precision.HIGHEST,
    ).astype(jnp.bfloat16)
    return (layer_out, grad_tokens, grad_gate[None], grad_up[None], grad_down[None])


def solution(mesh):
    return jax.shard_map(
        on_device,
        mesh=mesh,
        in_specs=(
            P(("expert", "hidden"), None),
            P(("expert", "hidden"), None),
            P(("expert", "hidden"), None),
            P(("expert", "hidden"), None),
            P("expert", None, "hidden"),
            P("expert", None, "hidden"),
            P("expert", "hidden", None),
        ),
        out_specs=(
            P(("expert", "hidden"), None),
            P(("expert", "hidden"), None),
            P("expert", None, "hidden"),
            P("expert", None, "hidden"),
            P("expert", "hidden", None),
        ),
        check_vma=False,
    )
```

profile of v0, /device:TPU:0, one launch (start us, length us, event | category | flops | bytes accessed | tf_op | source)
XLA Modules:
  0.0 226.8 jit_solution(520925246236391324)
XLA Ops:
  7.2 0.0 copy-start
  7.2 0.0 all-gather.3.cloned.1.call-start
  7.2 0.8 copy.30
  8.0 0.1 eq.29
  8.1 0.2 reduce_window_sum.11
  8.3 0.1 reduce_sum.30
  8.4 0.8 copy.32
  9.2 0.1 convert_reduce_fusion
  9.3 0.2 convolution_convert_fusion.1
  9.5 0.8 broadcast_in_dim_reshape.7
  10.3 0.0 all-gather.3.cloned.1.call-update
  10.3 0.0 all-gather.5.cloned.1.call-start
  10.3 1.3 convolution_convert_fusion
  11.7 0.8 broadcast_in_dim_reshape.8
  12.4 0.0 all-gather.5.cloned.1.call-update
  12.4 25.8 %all-gather.3.cloned.1.call-done = bf16[8,4,4,6144]{3,2,1,0:T(4,128)(2,1)} async-done(((bf16[1,4,4,6144]{3,2,1,0:T(4,128)(2,1)}), bf16[8,4,4,6144]{3,2,1,0:T(4,128)(2,1)}) %all-gather.3.cloned.1.call-update) | async-done | bytes 1572880 | tf_op jit(solution)/shard_map/all_gather | solution.py:35
  38.2 3.3 %copy.33 = bf16[8,4,4,6144]{3,2,0,1:T(4,128)(2,1)} copy(bf16[8,4,4,6144]{3,2,1,0:T(4,128)(2,1)} %all-gather.3.cloned.1.call-done) | data formatting | bytes 3145728 | tf_op jit(solution)/shard_map/all_gather | solution.py:35
  41.5 3.6 %all-to-all-start = ((bf16[8,4,4,6144]{3,2,0,1:T(4,128)(2,1)}), bf16[8,4,4,6144]{3,2,0,1:T(4,128)(2,1)S(1)}, u32[]{:S(2)}, u32[]{:S(2)}) async-start(bf16[8,4,4,6144]{3,2,0,1:T(4,128)(2,1)} %copy.33), calls=%async_computation | async-start | bytes 3145728 | tf_op jit(solution)/shard_map/all_to_all | solution.py:39
  45.1 19.9 %all-gather.5.cloned.1.call-done = bf16[8,4,4,6144]{3,2,1,0:T(4,128)(2,1)} async-done(((bf16[1,4,4,6144]{3,2,1,0:T(4,128)(2,1)}), bf16[8,4,4,6144]{3,2,1,0:T(4,128)(2,1)}) %all-gather.5.cloned.1.call-update) | async-done | bytes 1572880 | tf_op jit(solution)/shard_map/all_gather | solution.py:36
  65.0 3.3 %copy.35 = bf16[8,4,4,6144]{3,2,0,1:T(4,128)(2,1)} copy(bf16[8,4,4,6144]{3,2,1,0:T(4,128)(2,1)} %all-gather.5.cloned.1.call-done) | data formatting | bytes 3145728 | tf_op jit(solution)/shard_map/all_gather | solution.py:36
  68.3 4.3 %all-to-all-start.2 = ((bf16[8,4,4,6144]{3,2,0,1:T(4,128)(2,1)}), bf16[8,4,4,6144]{3,2,0,1:T(4,128)(2,1)}, u32[]{:S(2)}, u32[]{:S(2)}) async-start(bf16[8,4,4,6144]{3,2,0,1:T(4,128)(2,1)} %copy.35), calls=%async_computation.3 | async-start | bytes 3145728 | tf_op jit(solution)/shard_map/all_to_all | solution.py:40
  72.6 0.0 reduce-scatter.5.cloned.1.call-start
  72.7 1.9 copy.34
  74.6 2.7 %reshape.48 = bf16[128,6144]{1,0:T(8,128)(2,1)S(1)} reshape(bf16[8,4,4,6144]{3,2,1,0:T(4,128)(2,1)} %copy.34) | data formatting | bytes 3145728 | tf_op jit(solution)/shard_map/reshape | solution.py:42
  77.3 15.4 %all-to-all-done.2 = bf16[8,4,4,6144]{3,2,0,1:T(4,128)(2,1)} async-done(((bf16[8,4,4,6144]{3,2,0,1:T(4,128)(2,1)}), bf16[8,4,4,6144]{3,2,0,1:T(4,128)(2,1)}, u32[]{:S(2)}, u32[]{:S(2)}) %all-to-all-start.2) | async-done | bytes 1572896 | tf_op jit(solution)/shard_map/all_to_all | solution.py:40
  92.6 3.3 %copy.36 = bf16[8,4,4,6144]{3,2,1,0:T(4,128)(2,1)} copy(bf16[8,4,4,6144]{3,2,0,1:T(4,128)(2,1)} %all-to-all-done.2) | data formatting | bytes 3145728 | tf_op jit(solution)/shard_map/all_to_all | solution.py:40
  95.9 2.9 %reshape.51 = bf16[128,6144]{1,0:T(8,128)(2,1)S(1)} reshape(bf16[8,4,4,6144]{3,2,1,0:T(4,128)(2,1)} %copy.36) | data formatting | bytes 3145728 | tf_op jit(solution)/shard_map/reshape | solution.py:43
  98.8 7.2 %fusion.6 = f32[128,1024]{1,0:T(8,128)} fusion(bf16[128,6144]{1,0:T(8,128)(2,1)S(1)} %reshape.48, bf16[1,6144,1024]{2,1,0:T(8,128)(2,1)} %param.12), kind=kOutput, calls=%fused_computation.6 | convolution fusion | flops 1610612736 | bytes 14680064 | tf_op jit(solution)/shard_map/dot_general | solution.py:48
  105.9 9.8 %fusion = f32[128,1024]{1,0:T(8,128)} fusion(bf16[128,6144]{1,0:T(8,128)(2,1)S(1)} %reshape.51, bf16[1,1024,6144]{2,1,0:T(8,128)(2,1)} %param.13), kind=kOutput, calls=%fused_computation | convolution fusion | flops 1610612736 | bytes 14680064 | tf_op jit(solution)/shard_map/dot_general | solution.py:62
  115.7 7.8 %multiply_convert_fusion.1 = (bf16[128,1024]{1,0:T(8,128)(2,1)S(1)}, bf16[128,1024]{1,0:T(8,128)(2,1)}, bf16[128,1024]{1,0:T(8,128)(2,1)}) fusion(f32[128,1024]{1,0:T(8,128)} %fusion, f32[128,1024]{1,0:T(8,128)} %fusion.6, bf16[128,6144]{1,0:T(8,128)(2,1)S(1)} %reshape.48, bf16[1,6144,1024]{2,1,0:T(8,128)(2,1)} %param.11), kind=kOutput, calls=%fused_computation.23 | convolution fusion | flops 1612709888 | bytes 15990784 | tf_op jit(solution)/shard_map/dot_general | solution.py:47
  123.5 6.9 %fusion.4 = f32[128,6144]{1,0:T(8,128)} fusion(bf16[128,1024]{1,0:T(8,128)(2,1)} %get-tuple-element.9, bf16[1,6144,1024]{2,1,0:T(8,128)(2,1)S(1)} %bitcast.49), kind=kOutput, calls=%fused_computation.4 | convolution fusion | flops 1610612736 | bytes 15990784 | tf_op jit(solution)/shard_map/dot_general | solution.py:78
  130.4 11.1 %fusion.15 = bf16[128,6144]{1,0:T(8,128)(2,1)} fusion(f32[128,6144]{1,0:T(8,128)} %fusion.4, bf16[128,1024]{1,0:T(8,128)(2,1)S(1)} %get-tuple-element.7, bf16[1,6144,1024]{2,1,0:T(8,128)(2,1)} %param.11), kind=kOutput, calls=%fused_computation.16 | convolution fusion | flops 1612185600 | bytes 17563648 | tf_op jit(solution)/shard_map/dot_general | solution.py:76
  141.5 0.0 reduce-scatter.5.cloned.1.call-update
  141.5 0.0 reduce-scatter.3.cloned.1.call-start
  141.6 7.7 %fusion.18 = bf16[128,6144]{1,0:T(8,128)(2,1)} fusion(bf16[128,1024]{1,0:T(8,128)(2,1)} %get-tuple-element.8, bf16[1,1024,6144]{2,1,0:T(8,128)(2,1)} %param.13), kind=kOutput, calls=%fused_computation.17 | convolution fusion | flops 1611399168 | bytes 14417920 | tf_op jit(solution)/shard_map/dot_general | solution.py:52
  149.2 0.0 reduce-scatter.3.cloned.1.call-update
  149.2 7.6 %convert_bitcast_fusion.1 = bf16[1,6144,1024]{2,1,0:T(8,128)(2,1)} fusion(bf16[128,6144]{1,0:T(8,128)(2,1)S(1)} %reshape.48, bf16[128,1024]{1,0:T(8,128)(2,1)} %get-tuple-element.9), kind=kOutput, calls=%fused_computation.13 | convolution fusion | flops 1616904192 | bytes 14417920 | tf_op jit(solution)/shard_map/dot_general | solution.py:73
  156.8 6.6 %convert_bitcast_fusion.2 = bf16[1,6144,1024]{2,1,0:T(8,128)(2,1)} fusion(bf16[128,6144]{1,0:T(8,128)(2,1)S(1)} %reshape.48, bf16[128,1024]{1,0:T(8,128)(2,1)S(1)} %get-tuple-element.7), kind=kOutput, calls=%fused_computation.14 | convolution fusion | flops 1616904192 | bytes 14417920 | tf_op jit(solution)/shard_map/dot_general | solution.py:70
  163.4 11.1 %reduce-scatter.5.cloned.1.call-done = bf16[16,6144]{1,0:T(8,128)(2,1)} async-done(((bf16[128,6144]{1,0:T(8,128)(2,1)}), bf16[16,6144]{1,0:T(8,128)(2,1)}) %reduce-scatter.5.cloned.1.call-update) | async-done | bytes 196624 | tf_op jit(solution)/shard_map/reduce_scatter | solution.py:77
  174.6 1.7 reshape.52
  176.3 3.5 %all-to-all-start.3 = ((bf16[4,4,6144]{2,1,0:T(4,128)(2,1)}), bf16[4,4,6144]{2,1,0:T(4,128)(2,1)S(1)}, u32[]{:S(2)}, u32[]{:S(2)}) async-start(bf16[4,4,6144]{2,1,0:T(4,128)(2,1)} %reshape.52), calls=%async_computation.5 | async-start | bytes 393216 | tf_op jit(solution)/shard_map/all_to_all | solution.py:86
  179.8 7.6 %convert_bitcast_fusion = bf16[1,1024,6144]{2,1,0:T(8,128)(2,1)} fusion(bf16[128,1024]{1,0:T(8,128)(2,1)} %get-tuple-element.8, bf16[128,6144]{1,0:T(8,128)(2,1)S(1)} %reshape.51), kind=kOutput, calls=%fused_computation.12 | convolution fusion | flops 1616904192 | bytes 14417920 | tf_op jit(solution)/shard_map/dot_general | solution.py:67
  187.4 21.5 %reduce-scatter.3.cloned.1.call-done = bf16[16,6144]{1,0:T(8,128)(2,1)} async-done(((bf16[128,6144]{1,0:T(8,128)(2,1)}), bf16[16,6144]{1,0:T(8,128)(2,1)}) %reduce-scatter.3.cloned.1.call-update) | async-done | bytes 196624 | tf_op jit(solution)/shard_map/reduce_scatter | solution.py:51
  208.8 1.7 reshape.49
  210.5 3.6 %all-to-all-start.1 = ((bf16[4,4,6144]{2,1,0:T(4,128)(2,1)}), bf16[4,4,6144]{2,1,0:T(4,128)(2,1)S(1)}, u32[]{:S(2)}, u32[]{:S(2)}) async-start(bf16[4,4,6144]{2,1,0:T(4,128)(2,1)} %reshape.49), calls=%async_computation.2 | async-start | bytes 393216 | tf_op jit(solution)/shard_map/all_to_all | solution.py:58
  214.2 0.9 convolution_convert_fusion.2
  215.0 4.3 %all-to-all-done.1 = bf16[4,4,6144]{2,1,0:T(4,128)(2,1)S(1)} async-done(((bf16[4,4,6144]{2,1,0:T(4,128)(2,1)}), bf16[4,4,6144]{2,1,0:T(4,128)(2,1)S(1)}, u32[]{:S(2)}, u32[]{:S(2)}) %all-to-all-start.1) | async-done | bytes 196640 | tf_op jit(solution)/shard_map/all_to_all | solution.py:58
  219.4 0.9 convolution_convert_fusion.3
  (17 shorter events, 0.2 us)
Async XLA Ops:
  7.2 2.1 copy-start
  7.2 31.0 %all-gather.3.cloned.1.call-start = ((), (), s32[]{:S(2)}) async-start(), calls=%async_computation.6 | async-start | bytes 1769472 | tf_op jit(solution)/shard_map/all_gather | solution.py:35
  10.3 54.7 %all-gather.5.cloned.1.call-start = ((), (), s32[]{:S(2)}) async-start(), calls=%async_computation.8 | async-start | bytes 1769472 | tf_op jit(solution)/shard_map/all_gather | solution.py:36
  41.5 26.8 %all-to-all-start = ((bf16[8,4,4,6144]{3,2,0,1:T(4,128)(2,1)}), bf16[8,4,4,6144]{3,2,0,1:T(4,128)(2,1)S(1)}, u32[]{:S(2)}, u32[]{:S(2)}) async-start(bf16[8,4,4,6144]{3,2,0,1:T(4,128)(2,1)} %copy.33), calls=%async_computation | async-start | bytes 3145728 | tf_op jit(solution)/shard_map/all_to_all | solution.py:39
  68.3 24.3 %all-to-all-start.2 = ((bf16[8,4,4,6144]{3,2,0,1:T(4,128)(2,1)}), bf16[8,4,4,6144]{3,2,0,1:T(4,128)(2,1)}, u32[]{:S(2)}, u32[]{:S(2)}) async-start(bf16[8,4,4,6144]{3,2,0,1:T(4,128)(2,1)} %copy.35), calls=%async_computation.3 | async-start | bytes 3145728 | tf_op jit(solution)/shard_map/all_to_all | solution.py:40
  72.6 101.9 %reduce-scatter.5.cloned.1.call-start = ((), (), s32[]{:S(2)}) async-start(), calls=%async_computation.9 | async-start | bytes 1769472 | tf_op jit(solution)/shard_map/reduce_scatter | solution.py:77
  105.9 17.6 %slice-start = ((s8[12582912]{0:T(1024)(128)(4,1)}), s8[4194304]{0:T(1024)(128)(4,1)S(1)}, s32[]{:S(2)}) async-start(s8[12582912]{0:T(1024)(128)(4,1)} %bitcast.48), calls=%async_computation.10 | async-start | bytes 8388608
  105.9 17.6 %slice-start.1 = ((s8[12582912]{0:T(1024)(128)(4,1)}), s8[4194304]{0:T(1024)(128)(4,1)S(1)}, s32[]{:S(2)}) async-start(s8[12582912]{0:T(1024)(128)(4,1)} %bitcast.48), calls=%async_computation.11 | async-start | bytes 8388608
  115.7 7.8 %slice-start.2 = ((s8[12582912]{0:T(1024)(128)(4,1)}), s8[4194304]{0:T(1024)(128)(4,1)S(1)}, s32[]{:S(2)}) async-start(s8[12582912]{0:T(1024)(128)(4,1)} %bitcast.48), calls=%async_computation.12 | async-start | bytes 8388608
  141.5 67.3 %reduce-scatter.3.cloned.1.call-start = ((), (), s32[]{:S(2)}) async-start(), calls=%async_computation.7 | async-start | bytes 1769472 | tf_op jit(solution)/shard_map/reduce_scatter | solution.py:51
  176.3 34.3 %all-to-all-start.3 = ((bf16[4,4,6144]{2,1,0:T(4,128)(2,1)}), bf16[4,4,6144]{2,1,0:T(4,128)(2,1)S(1)}, u32[]{:S(2)}, u32[]{:S(2)}) async-start(bf16[4,4,6144]{2,1,0:T(4,128)(2,1)} %reshape.52), calls=%async_computation.5 | async-start | bytes 393216 | tf_op jit(solution)/shard_map/all_to_all | solution.py:86
  179.7 40.5 %copy-start.1 = (bf16[6,6144]{1,0:T(8,128)(2,1)S(1)}, bf16[6,6144]{1,0:T(8,128)(2,1)}, u32[]{:S(2)}) copy-start(bf16[6,6144]{1,0:T(8,128)(2,1)} %param.7) | copy-start | bytes 221188
  210.5 8.8 %all-to-all-start.1 = ((bf16[4,4,6144]{2,1,0:T(4,128)(2,1)}), bf16[4,4,6144]{2,1,0:T(4,128)(2,1)S(1)}, u32[]{:S(2)}, u32[]{:S(2)}) async-start(bf16[4,4,6144]{2,1,0:T(4,128)(2,1)} %reshape.49), calls=%async_computation.2 | async-start | bytes 393216 | tf_op jit(solution)/shard_map/all_to_all | solution.py:58
Sparse Core Ops, SparseCore 0:
  10.4 27.7 all-gather.2
  40.4 24.5 all-gather.4
  141.6 32.8 reduce-scatter.4
  176.7 32.0 reduce-scatter.2
where the time goes:
time: 228 us; the launch traced here: 227 us
  waiting for transfers between devices  98 us (43%)
  matrix products  75.4 us (33%)
  local copies, waits for them, and re-layouts  23.9 us (10%)
  starting transfers between devices  15.3 us (7%)
  between operations  13.9 us (6%)
    all_gather x1, waiting for transfers between devices, on_device(): lax.all_gather(send_in[None], 'hidden', axis=0, tiled=True)  25.8 us
    reduce_scatter x1, waiting for transfers between devices, on_device(): lax.psum_scatter(jnp.dot(hidden, down_w, preferred_element_type=jnp.float...  21.5 us
    all_gather x1, waiting for transfers between devices, on_device(): lax.all_gather(send_grad[None], 'hidden', axis=0, tiled=True)  19.9 us
    all_to_all x1, waiting for transfers between devices, on_device(): lax.all_to_all(grouped[1], 'expert', split_axis=1, concat_axis=1, tiled=T...  15.4 us
    reduce_scatter x1, waiting for transfers between devices, on_device(): lax.psum_scatter((first + jnp.dot(grad_pre_up, up_w.T, preferred_element_...  11.1 us
    dot_general x1, matrix products, on_device(): first = jnp.dot(grad_pre_gate, gate_w.T, preferred_element_type=jnp.float32)  11.1 us
    dot_general x1, matrix products, on_device(): jnp.dot(grad_rows, down_w.T, preferred_element_type=jnp.float32)  9.76 us
    dot_general x1, matrix products, on_device(): pre_gate = jnp.dot(expert_rows, gate_w, preferred_element_type=jnp.float32)  7.78 us
  transfers between devices with their start and end apart: 8, of which 6 were waited for; matrix products, arithmetic and copies ran while one was open for 21% of the time, Pallas kernels for 0%

commit v1 on v0

--- a/solution.py
+++ b/solution.py
@@ -1,13 +1,255 @@
+import functools
+
 import jax
 import jax.numpy as jnp
 from jax import lax
+from jax.experimental import pallas as pl
+from jax.experimental.pallas import tpu as pltpu
 from jax.sharding import PartitionSpec as P
+
+CHUNKS = 4
+META = 128
+MESH = pl.DeviceIdType.MESH
+
+
+def gather_kernel(experts, hidden, blk_ref, out_ref, send_sem, recv_sem):
+    e = lax.axis_index("expert")
+    h = lax.axis_index("hidden")
+    chips = hidden // 2
+    chip, core = h // 2, h % 2
+    x, y = e % 2, e // 2
+    step_x, step_y = 1 - 2 * x, 2 - 4 * y
+    near = e + (1 - core) * step_x + core * step_y
+    far = e + core * step_x + (1 - core) * step_y
+    diag = e + step_x + step_y
+    sibling = h + 1 - 2 * core
+
+    def slot(ee, c):
+        return (c * 2 + core) * experts + ee
+
+    def copy(kind, ident, dev, own=False):
+        return pltpu.make_async_remote_copy(
+            src_ref=blk_ref if own else out_ref.at[ident],
+            dst_ref=out_ref.at[ident],
+            send_sem=send_sem.at[kind, ident],
+            recv_sem=recv_sem.at[ident],
+            device_id=dev,
+            device_id_type=MESH,
+        )
+
+    up, down = (e, h + 2), (e, h - 2)
+    to_near, to_far, to_sib = (near, h), (far, h), (e, sibling)
+    has_up, has_down = chip < chips - 1, chip > 0
+
+    barrier = pltpu.get_barrier_semaphore()
+    for dev in (to_near, to_far, to_sib):
+        pl.semaphore_signal(barrier, inc=1, device_id=dev, device_id_type=MESH)
+
+    @pl.when(has_up)
+    def _():
+        pl.semaphore_signal(barrier, inc=1, device_id=up, device_id_type=MESH)
+
+    @pl.when(has_down)
+    def _():
+        pl.semaphore_signal(barrier, inc=1, device_id=down, device_id_type=MESH)
+
+    pl.semaphore_wait(barrier, 3 + has_up.astype(jnp.int32) + has_down.astype(jnp.int32))
+
+    def publish(ident, own=False):
+        copy(2, ident, to_near, own).start()
+        copy(3, ident, to_far, own).start()
+        copy(4, ident, to_sib, own).start()
+
+    def plane(c):
+        a, b, d = slot(near, c), slot(far, c), slot(diag, c)
+        copy(0, a, to_near).wait_recv()
+        copy(3, a, to_far).start()
+        copy(4, a, to_sib).start()
+        copy(0, b, to_far).wait_recv()
+        copy(4, b, to_sib).start()
+        copy(0, d, to_near).wait_recv()
+        copy(4, d, to_sib).start()
+
+    mine = slot(e, chip)
+
+    @pl.when(has_up)
+    def _():
+        copy(0, mine, up, True).start()
+
+    @pl.when(has_down)
+    def _():
+        copy(1, mine, down, True).start()
+
+    publish(mine, True)
+    out_ref[pl.ds(mine, 1)] = blk_ref[...][None]
+
+    for k in range(1, chips):
+
+        @pl.when(chip >= k)
+        def _():
+            ident = slot(e, chip - k)
+            copy(0, ident, up).wait_recv()
+
+            @pl.when(has_up)
+            def _():
+                copy(0, ident, up).start()
+
+            publish(ident)
+
+        @pl.when(chip + k < chips)
+        def _():
+            ident = slot(e, chip + k)
+            copy(1, ident, down).wait_recv()
+
+            @pl.when(has_down)
+            def _():
+                copy(1, ident, down).start()
+
+            publish(ident)
+
+        if k == 1:
+            plane(chip)
+        else:
+
+            @pl.when(chip >= k - 1)
+            def _():
+                plane(chip - (k - 1))
+
+            @pl.when(chip + (k - 1) < chips)
+            def _():
+                plane(chip + (k - 1))
+
+    if chips == 1:
+        plane(chip)
+    else:
+
+        @pl.when(chip >= chips - 1)
+        def _():
+            plane(chip - (chips - 1))
+
+        @pl.when(chip + (chips - 1) < chips)
+        def _():
+            plane(chip + (chips - 1))
+
+    for c in range(chips):
+        for ee in range(experts):
+            ident = (c * 2 + 1 - core) * experts + ee
+            copy(4, ident, to_sib).wait_recv()
+    for c in range(chips):
+        ident = slot(e, c)
+
+        @pl.when(has_up & (chip >= c))
+        def _():
+            copy(0, ident, up).wait_send()
+
+        @pl.when(has_down & (chip <= c))
+        def _():
+            copy(1, ident, down).wait_send()
+
+        copy(2, ident, to_near).wait_send()
+        copy(3, ident, to_far).wait_send()
+        copy(3, slot(near, c), to_far).wait_send()
+        for ee in range(experts):
+            copy(4, slot(ee, c), to_sib).wait_send()
+
+
+def gather_blocks(block, experts, hidden):
+    count = experts * hidden
+    return pl.pallas_call(
+        functools.partial(gather_kernel, experts, hidden),
+        out_shape=jax.ShapeDtypeStruct((count,) + block.shape, block.dtype),
+        in_specs=[pl.BlockSpec(memory_space=pltpu.VMEM)],
+        out_specs=pl.BlockSpec(memory_space=pltpu.VMEM),
+        scratch_shapes=[
+            pltpu.SemaphoreType.DMA((5, count)),
+            pltpu.SemaphoreType.DMA((count,)),
+        ],
+        compiler_params=pltpu.CompilerParams(
+            collective_id=0, has_side_effects=True, vmem_limit_bytes=48 * 1024 * 1024
+        ),
+    )(block)
+
+
+def place_kernel(rows, width, pick_ref, scale_ref, all_ref, in_ref, grad_ref):
+    got = jnp.dot(pick_ref[0, 0], all_ref[:, :width], preferred_element_type=jnp.float32)
+    in_ref[...] = got[:rows].astype(jnp.bfloat16)
+    grad_ref[...] = (got[rows:] * scale_ref[...]).astype(jnp.bfloat16)
+
+
+def dispatch(tokens, routes, gate_probs, cotangent, experts, hidden, capacity):
+    count, width = tokens.shape
+    part = width // CHUNKS
+    rows2 = 2 * count
+    both = jnp.concatenate([tokens, cotangent], axis=0)
+    body = both.reshape(rows2, CHUNKS, part).transpose(1, 0, 2)
+    high = lax.reduce_precision(gate_probs, 8, 7)
+    rest = gate_probs - high
+    middle = lax.reduce_precision(rest, 8, 7)
+    low = rest - middle
+    meta = jnp.concatenate(
+        [routes.astype(jnp.float32), high, middle, low], axis=1
+    ).astype(jnp.bfloat16)
+    meta = jnp.pad(meta, ((0, rows2 - count), (0, META - 8)))
+    meta = jnp.broadcast_to(meta[None], (CHUNKS, rows2, META))
+    block = jnp.concatenate([body, meta], axis=2).reshape(CHUNKS * rows2, part + META)
+    gathered = gather_blocks(block, experts, hidden)
+    blocks = experts * hidden
+    meta = gathered[:, :count, part : part + 8].astype(jnp.float32)
+    ids = meta[:, :, :2]
+    probs = meta[:, :, 2:4] + meta[:, :, 4:6] + meta[:, :, 6:8]
+    here = lax.axis_index("expert").astype(jnp.float32)
+    hits = (ids.reshape(blocks, 2 * count) == here).astype(jnp.int32)
+    order = jnp.tril(jnp.ones((2 * count, 2 * count), jnp.int32), -1)
+    ranks = jnp.sum(hits[:, None, :] * order[None], axis=2)
+    pick = (hits[:, None, :] == 1) & (
+        ranks[:, None, :] == jnp.arange(capacity, dtype=jnp.int32)[None, :, None]
+    )
+    pick = pick.astype(jnp.float32).reshape(blocks, capacity, count, 2)
+    scale = jnp.sum(pick * probs[:, None], axis=(2, 3)).reshape(blocks * capacity, 1)
+    pick = jnp.sum(pick, axis=3).reshape(blocks * capacity, count)
+    size = 16 if blocks % 16 == 0 else blocks
+    groups, rows = blocks // size, size * capacity
+    width_all = size * CHUNKS * rows2
+    col = jnp.arange(width_all, dtype=jnp.int32)
+    col_tok = col % count
+    col_kind = (col // count) % 2
+    col_chunk = (col // rows2) % CHUNKS
+    col_block = col // (rows2 * CHUNKS)
+    spread = (col_tok[None, :] == jnp.arange(count, dtype=jnp.int32)[:, None]).astype(jnp.bfloat16)
+    tiled = jnp.dot(pick.astype(jnp.bfloat16), spread, preferred_element_type=jnp.float32)
+    tiled = tiled.reshape(groups, rows, width_all)
+    own = col_block[None, :] == (jnp.arange(rows, dtype=jnp.int32) // capacity)[:, None]
+    tiled = jnp.where(own[None], tiled, 0.0).astype(jnp.bfloat16)
+    chunk_ok = col_chunk[None, :] == jnp.arange(CHUNKS, dtype=jnp.int32)[:, None]
+    kind_ok = col_kind[None, :] == jnp.arange(2, dtype=jnp.int32)[:, None]
+    keep = (chunk_ok[:, None, :] & kind_ok[None]).astype(jnp.bfloat16)
+    pick_all = keep[None, :, :, None, :] * tiled[:, None, None]
+    pick_all = pick_all.reshape(groups, CHUNKS, 2 * rows, width_all)
+    flat = gathered.reshape(groups * width_all, part + META)
+    shape = jax.ShapeDtypeStruct((groups * rows, width), jnp.bfloat16)
+    return pl.pallas_call(
+        functools.partial(place_kernel, rows, part),
+        grid=(groups, CHUNKS),
+        out_shape=(shape, shape),
+        in_specs=[
+            pl.BlockSpec((1, 1, 2 * rows, width_all), lambda g, c: (g, c, 0, 0)),
+            pl.BlockSpec((rows, 1), lambda g, c: (g, 0)),
+            pl.BlockSpec((width_all, part + META), lambda g, c: (g, 0)),
+        ],
+        out_specs=(
+            pl.BlockSpec((rows, part), lambda g, c: (g, c)),
+            pl.BlockSpec((rows, part), lambda g, c: (g, c)),
+        ),
+        compiler_params=pltpu.CompilerParams(vmem_limit_bytes=40 * 1024 * 1024),
+    )(pick_all, scale, flat)
 
 
 def slot_table(route_ids, experts, capacity):
     flat_ids = route_ids.reshape(-1)
     hits = (flat_ids[:, None] == jnp.arange(experts, dtype=jnp.int32)[None, :]).astype(jnp.int32)
-    before = jnp.cumsum(hits, axis=0) - hits
+    pairs = flat_ids.shape[0]
+    earlier = jnp.tril(jnp.ones((pairs, pairs), jnp.int32), -1)
+    before = jnp.sum(earlier[:, :, None] * hits[None], axis=1)
     ranks = jnp.sum(before * hits, axis=1)
     slot_ids = flat_ids * capacity + ranks
     table = (slot_ids[:, None] == jnp.arange(experts * capacity, dtype=jnp.int32)[None, :]).astype(
@@ -23,24 +265,9 @@
     table = slot_table(routes, experts, capacity)
     placed = jnp.sum(table, axis=1)
     weighted = jnp.sum(table * gate_probs[:, :, None], axis=1)
-    send_in = jnp.dot(
-        placed.T.astype(jnp.bfloat16), tokens, preferred_element_type=jnp.float32
-    ).astype(jnp.bfloat16)
-    send_grad = jnp.dot(
-        weighted.T, cotangent.astype(jnp.float32), precision=lax.Precision.HIGHEST
-    ).astype(jnp.bfloat16)
-    send_in = send_in.reshape(experts, capacity, width)
-    send_grad = send_grad.reshape(experts, capacity, width)
-    grouped = (
-        lax.all_gather(send_in[None], "hidden", axis=0, tiled=True),
-        lax.all_gather(send_grad[None], "hidden", axis=0, tiled=True),
-    )
-    arrived = (
-        lax.all_to_all(grouped[0], "expert", split_axis=1, concat_axis=1, tiled=True),
-        lax.all_to_all(grouped[1], "expert", split_axis=1, concat_axis=1, tiled=True),
-    )
-    expert_rows = arrived[0].reshape(-1, width)
-    grad_rows = arrived[1].reshape(-1, width)
+    expert_rows, grad_rows = dispatch(
+        tokens, routes, gate_probs, cotangent, experts, lax.axis_size("hidden"), capacity
+    )
     gate_w = w_gate[0]
     up_w = w_up[0]
     down_w = w_down[0]

time: 228 us -> 168 us (0.74)
  waiting for transfers between devices: 98 us -> 26.1 us
  Pallas kernels: 0 us -> 40.8 us
  local copies, waits for them, and re-layouts: 23.9 us -> 10.6 us
  matrix products: 75.4 us -> 64.5 us
  starting transfers between devices: 15.3 us -> 7.38 us
  other arithmetic: 0.32 us -> 3.78 us
    all_gather x2 -> x0, waiting for transfers between devices: 45.7 us -> none  [the longest x1 25.8 us: on_device(): lax.all_gather(send_in[None], 'hidden', axis=0, tiled=True)]
    pallas_call x0 -> x2, Pallas kernels: none -> 40.8 us  [the longest x1 36.6 us: gather_blocks(): pl.pallas_call(functools.partial(gather_kernel, experts, hidden), out_sha...]
    reduce_scatter x1, waiting for transfers between devices: 21.5 us -> 0.01 us  [on_device(): lax.psum_scatter(jnp.dot(hidden, down_w, preferred_element_type=jnp.float...]
    all_to_all x2 -> x0, waiting for transfers between devices: 15.4 us -> none  [the longest x1 15.4 us: on_device(): lax.all_to_all(grouped[1], 'expert', split_axis=1, concat_axis=1, tiled=T...]
    reduce_scatter x1, waiting for transfers between devices: 11.1 us -> 21.8 us  [on_device(): lax.psum_scatter((first + jnp.dot(grad_pre_up, up_w.T, preferred_element_...]
    all_to_all x2 -> x0, starting transfers between devices: 7.99 us -> none  [the longest x1 4.34 us: on_device(): lax.all_to_all(grouped[1], 'expert', split_axis=1, concat_axis=1, tiled=T...]
    all_gather x2 -> x0, local copies, waits for them, and re-layouts: 6.5 us -> none  [the longest x1 3.25 us: on_device(): lax.all_gather(send_grad[None], 'hidden', axis=0, tiled=True)]
    reshape x2 -> x4, local copies, waits for them, and re-layouts: 5.55 us -> 0.23 us  [the longest x2 0.11 us: dispatch(): body = both.reshape(rows2, CHUNKS, part).transpose(1, 0, 2)]
  transfers between devices with their start and end apart: 8 -> 4, of which waited for: 6 -> 2; matrix products, arithmetic and copies ran while one was open for 21% -> 27% of each run, Pallas kernels for 0% -> 0%
where the time goes in v1:
time: 168 us
  matrix products  64.5 us (38%)
  Pallas kernels  40.8 us (24%)
  waiting for transfers between devices  26.1 us (16%)
  between operations  14.4 us (9%)
  local copies, waits for them, and re-layouts  10.6 us (6%)
  starting transfers between devices  7.38 us (4%)
  other arithmetic  3.78 us (2%)
    pallas_call x1, Pallas kernels, gather_blocks(): pl.pallas_call(functools.partial(gather_kernel, experts, hidden), out_sha...  36.6 us
    reduce_scatter x1, waiting for transfers between devices, on_device(): lax.psum_scatter((first + jnp.dot(grad_pre_up, up_w.T, preferred_element_...  21.8 us
    dot_general x1, matrix products, on_device(): first = jnp.dot(grad_pre_gate, gate_w.T, preferred_element_type=jnp.float32)  10.2 us
    dot_general x1, matrix products, on_device(): jnp.dot(grad_rows, down_w.T, preferred_element_type=jnp.float32)  9.76 us
    dot_general x1, matrix products, on_device(): jnp.dot(grad_pre_up, up_w.T, preferred_element_type=jnp.float32)  8.82 us
    dot_general x1, matrix products, on_device(): pre_gate = jnp.dot(expert_rows, gate_w, preferred_element_type=jnp.float32)  8.1 us
    dot_general x1, matrix products, on_device(): jnp.dot(hidden.T, grad_rows, preferred_element_type=jnp.float32)  7.61 us
    dot_general x1, matrix products, on_device(): jnp.dot(expert_rows.T, grad_pre_up, preferred_element_type=jnp.float32)  6.6 us
  transfers between devices with their start and end apart: 4, of which 2 were waited for; matrix products, arithmetic and copies ran while one was open for 27% of the time, Pallas kernels for 0%

profile of v1, /device:TPU:0, one launch (start us, length us, event | category | flops | bytes accessed | tf_op | source)
XLA Modules:
  0.0 167.5 jit_solution(8008872563365551944)
XLA Ops:
  7.3 0.7 convert_convert_fusion
  8.0 0.7 reduce-precision_convert_fusion.1
  8.7 0.1 copy.58
  8.9 1.0 pad_maximum_fusion.1
  9.9 0.1 reshape.281
  10.1 36.6 %shard_map.110 = bf16[32,48,1664]{2,1,0:T(8,128)(2,1)S(1)} custom-call(bf16[48,1664]{1,0:T(8,128)(2,1)S(1)} %reshape.282.blk_ref), custom_call_target="tpu_custom_call" | custom-call | tf_op jit(solution)/shard_map/pallas_call | solution.py:158
  46.8 2.3 %copy-done = bf16[32,48,1664]{2,1,0:T(8,128)(2,1)} copy-done((bf16[32,48,1664]{2,1,0:T(8,128)(2,1)}, bf16[32,48,1664]{2,1,0:T(8,128)(2,1)S(1)}, u32[]{:S(2)}) %copy-start) | copy-done | bytes 5111832
  49.1 0.2 slice_add_fusion
  49.2 0.1 copy.54
  49.4 0.1 copy.50
  49.5 0.1 copy.51
  49.7 0.1 multiply_reduce_fusion
  49.8 0.1 copy.55
  49.9 0.1 reshape.291.scale_ref
  50.0 0.1 copy.52
  50.1 0.1 convert_element_type.102
  50.3 0.1 broadcast_compare_fusion
  50.4 0.3 fusion.21
  50.7 0.1 broadcast_multiply_fusion.pick_ref
  50.9 2.4 %copy-done.1 = bf16[32,48,1664]{2,1,0:T(8,128)(2,1)S(1)} copy-done((bf16[32,48,1664]{2,1,0:T(8,128)(2,1)S(1)}, bf16[32,48,1664]{2,1,0:T(8,128)(2,1)}, u32[]{:S(2)}) %copy-start.1) | copy-done | bytes 5111832
  53.3 4.2 %shard_map.111 = (bf16[128,6144]{1,0:T(8,128)(2,1)S(1)}, bf16[128,6144]{1,0:T(8,128)(2,1)S(1)}) custom-call(bf16[2,4,128,768]{3,2,1,0:T(8,128)(2,1)S(1)} %broadcast_multiply_fusion.pick_ref, f32[128,1]{1,0:T(8,128)S(1)} %reshape.291.scale_ref, bf16[1536,1664]{1,0:T(8,128)(2,1)S(1)} %bitcast.60), custom_call_target="tpu_custom_call" | custom-call | tf_op jit(solution)/shard_map/pallas_call | solution.py:230
  57.5 9.8 %fusion = f32[128,1024]{1,0:T(8,128)} fusion(bf16[128,6144]{1,0:T(8,128)(2,1)S(1)} %get-tuple-element.8, bf16[1,1024,6144]{2,1,0:T(8,128)(2,1)} %param.13), kind=kOutput, calls=%fused_computation | convolution fusion | flops 1610612736 | bytes 14680064 | tf_op jit(solution)/shard_map/dot_general | solution.py:289
  67.3 1.8 %fusion.6 = f32[128,1024]{1,0:T(8,128)S(1)} fusion(bf16[128,6144]{1,0:T(8,128)(2,1)S(1)} %get-tuple-element.7, bf16[1,6144,1024]{2,1,0:T(8,128)(2,1)S(1)} %copy-done.2), kind=kOutput, calls=%fused_computation.6 | convolution fusion | flops 1610612736 | bytes 14680064 | tf_op jit(solution)/shard_map/dot_general | solution.py:275
  69.2 8.1 %multiply_convert_fusion.1 = (bf16[128,1024]{1,0:T(8,128)(2,1)}, bf16[128,1024]{1,0:T(8,128)(2,1)S(1)}, bf16[128,1024]{1,0:T(8,128)(2,1)S(1)}) fusion(f32[128,1024]{1,0:T(8,128)S(1)} %copy-done.6, f32[128,1024]{1,0:T(8,128)S(1)} %fusion.6, bf16[128,6144]{1,0:T(8,128)(2,1)S(1)} %get-tuple-element.7, bf16[1,6144,1024]{2,1,0:T(8,128)(2,1)} %param.11), kind=kOutput, calls=%fused_computation.24 | convolution fusion | flops 1612709888 | bytes 15990784 | tf_op jit(solution)/shard_map/dot_general | solution.py:274
  77.3 0.7 copy-done.5
  78.0 3.0 %fusion.18 = bf16[128,6144]{1,0:T(8,128)(2,1)} fusion(bf16[128,1024]{1,0:T(8,128)(2,1)S(1)} %get-tuple-element.16, bf16[1,1024,6144]{2,1,0:T(8,128)(2,1)S(1)} %bitcast.62), kind=kOutput, calls=%fused_computation.17 | convolution fusion | flops 1611399168 | bytes 14417920 | tf_op jit(solution)/shard_map/dot_general | solution.py:279
  81.0 0.2 reduce-scatter.5.cloned.1.call-start
  81.3 8.8 %fusion.4 = f32[128,6144]{1,0:T(8,128)S(1)} fusion(bf16[128,1024]{1,0:T(8,128)(2,1)S(1)} %get-tuple-element.17, bf16[1,6144,1024]{2,1,0:T(8,128)(2,1)} %param.12), kind=kOutput, calls=%fused_computation.4 | convolution fusion | flops 1610612736 | bytes 15990784 | tf_op jit(solution)/shard_map/dot_general | solution.py:305
  90.1 10.2 %fusion.15 = bf16[128,6144]{1,0:T(8,128)(2,1)} fusion(f32[128,6144]{1,0:T(8,128)S(1)} %fusion.4, bf16[128,1024]{1,0:T(8,128)(2,1)S(1)} %copy-done.3, bf16[1,6144,1024]{2,1,0:T(8,128)(2,1)} %param.11), kind=kOutput, calls=%fused_computation.16 | convolution fusion | flops 1612185600 | bytes 17563648 | tf_op jit(solution)/shard_map/dot_general | solution.py:303
  100.3 0.1 copy.42
  100.4 0.1 eq.142
  100.6 0.1 copy.44
  100.7 0.3 multiply_reduce_fusion.1
  100.9 0.2 select_reduce_fusion.1
  101.1 0.1 reduce_sum.67
  101.2 7.6 %convert_bitcast_fusion = bf16[1,1024,6144]{2,1,0:T(8,128)(2,1)} fusion(bf16[128,1024]{1,0:T(8,128)(2,1)} %copy-done.5, bf16[128,6144]{1,0:T(8,128)(2,1)S(1)} %get-tuple-element.8), kind=kOutput, calls=%fused_computation.12 | convolution fusion | flops 1616904192 | bytes 14417920 | tf_op jit(solution)/shard_map/dot_general | solution.py:294
  108.8 6.6 %convert_bitcast_fusion.2 = bf16[1,6144,1024]{2,1,0:T(8,128)(2,1)} fusion(bf16[128,6144]{1,0:T(8,128)(2,1)S(1)} %get-tuple-element.7, bf16[128,1024]{1,0:T(8,128)(2,1)S(1)} %copy-done.4), kind=kOutput, calls=%fused_computation.14 | convolution fusion | flops 1616904192 | bytes 14417920 | tf_op jit(solution)/shard_map/dot_general | solution.py:297
  115.4 6.6 %convert_bitcast_fusion.1 = bf16[1,6144,1024]{2,1,0:T(8,128)(2,1)} fusion(bf16[128,6144]{1,0:T(8,128)(2,1)S(1)} %get-tuple-element.7, bf16[128,1024]{1,0:T(8,128)(2,1)S(1)} %get-tuple-element.17), kind=kOutput, calls=%fused_computation.13 | convolution fusion | flops 1616904192 | bytes 14417920 | tf_op jit(solution)/shard_map/dot_general | solution.py:300
  122.0 1.7 %reshape.285 = bf16[4,4,6144]{2,1,0:T(4,128)(2,1)} reshape(bf16[16,6144]{1,0:T(8,128)(2,1)} %reduce-scatter.3.cloned.1.call-done) | data formatting | bytes 393216 | tf_op jit(solution)/shard_map/reshape | solution.py:284
  123.7 3.4 %all-to-all-start = ((bf16[4,4,6144]{2,1,0:T(4,128)(2,1)}), bf16[4,4,6144]{2,1,0:T(4,128)(2,1)S(1)}, u32[]{:S(2)}, u32[]{:S(2)}) async-start(bf16[4,4,6144]{2,1,0:T(4,128)(2,1)} %reshape.285), calls=%async_computation.1 | async-start | bytes 393216 | tf_op jit(solution)/shard_map/all_to_all | solution.py:285
  127.1 0.1 copy.46
  127.2 0.1 convert_reduce_fusion.1
  127.3 21.8 %reduce-scatter.5.cloned.1.call-done = bf16[16,6144]{1,0:T(8,128)(2,1)} async-done(((bf16[128,6144]{1,0:T(8,128)(2,1)}), bf16[16,6144]{1,0:T(8,128)(2,1)}) %reduce-scatter.5.cloned.1.call-update) | async-done | bytes 196624 | tf_op jit(solution)/shard_map/reduce_scatter | solution.py:304
  149.1 1.7 %reshape.287 = bf16[4,4,6144]{2,1,0:T(4,128)(2,1)} reshape(bf16[16,6144]{1,0:T(8,128)(2,1)} %reduce-scatter.5.cloned.1.call-done) | data formatting | bytes 393216 | tf_op jit(solution)/shard_map/reshape | solution.py:312
  150.8 3.8 %all-to-all-start.1 = ((bf16[4,4,6144]{2,1,0:T(4,128)(2,1)}), bf16[4,4,6144]{2,1,0:T(4,128)(2,1)S(1)}, u32[]{:S(2)}, u32[]{:S(2)}) async-start(bf16[4,4,6144]{2,1,0:T(4,128)(2,1)} %reshape.287), calls=%async_computation.3 | async-start | bytes 393216 | tf_op jit(solution)/shard_map/all_to_all | solution.py:313
  154.6 0.9 convolution_convert_fusion.1
  155.5 4.3 %all-to-all-done.1 = bf16[4,4,6144]{2,1,0:T(4,128)(2,1)S(1)} async-done(((bf16[4,4,6144]{2,1,0:T(4,128)(2,1)}), bf16[4,4,6144]{2,1,0:T(4,128)(2,1)S(1)}, u32[]{:S(2)}, u32[]{:S(2)}) %all-to-all-start.1) | async-done | bytes 196640 | tf_op jit(solution)/shard_map/all_to_all | solution.py:313
  159.8 0.9 convolution_convert_fusion
  (54 shorter events, 0.8 us)
Async XLA Ops:
  7.2 114.9 %reduce-scatter.3.cloned.1.call-start = ((), (), s32[]{:S(2)}) async-start(), calls=%async_computation.4 | async-start | bytes 1769472 | tf_op jit(solution)/shard_map/reduce_scatter | solution.py:278
  46.8 2.3 %copy-start = (bf16[32,48,1664]{2,1,0:T(8,128)(2,1)}, bf16[32,48,1664]{2,1,0:T(8,128)(2,1)S(1)}, u32[]{:S(2)}) copy-start(bf16[32,48,1664]{2,1,0:T(8,128)(2,1)S(1)} %shard_map.110) | copy-start | bytes 15335428
  50.9 2.5 %copy-start.1 = (bf16[32,48,1664]{2,1,0:T(8,128)(2,1)S(1)}, bf16[32,48,1664]{2,1,0:T(8,128)(2,1)}, u32[]{:S(2)}) copy-start(bf16[32,48,1664]{2,1,0:T(8,128)(2,1)} %copy-done) | copy-start | bytes 15335428
  57.5 9.8 %copy-start.2 = (bf16[1,6144,1024]{2,1,0:T(8,128)(2,1)S(1)}, bf16[1,6144,1024]{2,1,0:T(8,128)(2,1)}, u32[]{:S(2)}) copy-start(bf16[1,6144,1024]{2,1,0:T(8,128)(2,1)} %param.12) | copy-start | bytes 37748740
  67.3 1.9 %copy-start.6 = (f32[128,1024]{1,0:T(8,128)S(1)}, f32[128,1024]{1,0:T(8,128)}, u32[]{:S(2)}) copy-start(f32[128,1024]{1,0:T(8,128)} %fusion) | copy-start | bytes 1572868
  67.3 10.7 %slice-start = ((s8[12582912]{0:T(1024)(128)(4,1)}), s8[4194304]{0:T(1024)(128)(4,1)S(1)}, s32[]{:S(2)}) async-start(s8[12582912]{0:T(1024)(128)(4,1)} %bitcast.61), calls=%async_computation.6 | async-start | bytes 8388608
  67.3 10.7 %slice-start.1 = ((s8[12582912]{0:T(1024)(128)(4,1)}), s8[4194304]{0:T(1024)(128)(4,1)S(1)}, s32[]{:S(2)}) async-start(s8[12582912]{0:T(1024)(128)(4,1)} %bitcast.61), calls=%async_computation.7 | async-start | bytes 8388608
  69.2 8.8 %slice-start.2 = ((s8[12582912]{0:T(1024)(128)(4,1)}), s8[4194304]{0:T(1024)(128)(4,1)S(1)}, s32[]{:S(2)}) async-start(s8[12582912]{0:T(1024)(128)(4,1)} %bitcast.61), calls=%async_computation.8 | async-start | bytes 8388608
  77.3 0.7 copy-start.5
  81.0 68.1 %reduce-scatter.5.cloned.1.call-start = ((), (), s32[]{:S(2)}) async-start(), calls=%async_computation.5 | async-start | bytes 1769472 | tf_op jit(solution)/shard_map/reduce_scatter | solution.py:304
  81.3 8.8 %copy-start.3 = (bf16[128,1024]{1,0:T(8,128)(2,1)S(1)}, bf16[128,1024]{1,0:T(8,128)(2,1)}, u32[]{:S(2)}) copy-start(bf16[128,1024]{1,0:T(8,128)(2,1)} %get-tuple-element.15) | copy-start | bytes 786436
  90.1 10.2 %copy-start.8 = (s32[6,2]{0,1:T(2,128)S(1)}, s32[6,2]{0,1:T(2,128)}, u32[]{:S(2)}) copy-start(s32[6,2]{0,1:T(2,128)} %param.8) | copy-start | bytes 148
  101.2 7.6 %copy-start.4 = (bf16[128,1024]{1,0:T(8,128)(2,1)S(1)}, bf16[128,1024]{1,0:T(8,128)(2,1)}, u32[]{:S(2)}) copy-start(bf16[128,1024]{1,0:T(8,128)(2,1)} %get-tuple-element.15) | copy-start | bytes 786436
  115.4 11.7 %copy-start.7 = (f32[6,2]{0,1:T(2,128)S(1)}, f32[6,2]{0,1:T(2,128)}, u32[]{:S(2)}) copy-start(f32[6,2]{0,1:T(2,128)} %param.9) | copy-start | bytes 148
  123.7 27.1 %all-to-all-start = ((bf16[4,4,6144]{2,1,0:T(4,128)(2,1)}), bf16[4,4,6144]{2,1,0:T(4,128)(2,1)S(1)}, u32[]{:S(2)}, u32[]{:S(2)}) async-start(bf16[4,4,6144]{2,1,0:T(4,128)(2,1)} %reshape.285), calls=%async_computation.1 | async-start | bytes 393216 | tf_op jit(solution)/shard_map/all_to_all | solution.py:285
  150.8 8.9 %all-to-all-start.1 = ((bf16[4,4,6144]{2,1,0:T(4,128)(2,1)}), bf16[4,4,6144]{2,1,0:T(4,128)(2,1)S(1)}, u32[]{:S(2)}, u32[]{:S(2)}) async-start(bf16[4,4,6144]{2,1,0:T(4,128)(2,1)} %reshape.287), calls=%async_computation.3 | async-start | bytes 393216 | tf_op jit(solution)/shard_map/all_to_all | solution.py:313
Sparse Core Ops, SparseCore 0:
  81.1 33.1 reduce-scatter.2
  116.7 32.3 reduce-scatter.4

commit v2 on v1

--- a/solution.py
+++ b/solution.py
@@ -244,6 +244,49 @@
     )(pick_all, scale, flat)
 
 
+def hidden_kernel(x_ref, g_ref, gate_ref, up_ref, down_ref, h_ref, da_ref, du_ref):
+    pre = jnp.dot(x_ref[...], gate_ref[0], preferred_element_type=jnp.float32)
+    up = jnp.dot(x_ref[...], up_ref[0], preferred_element_type=jnp.float32)
+    grad = lax.dot_general(
+        g_ref[...],
+        down_ref[0],
+        (((1,), (1,)), ((), ())),
+        preferred_element_type=jnp.float32,
+    )
+    sig = jax.nn.sigmoid(pre)
+    h_ref[...] = (pre * sig * up).astype(jnp.bfloat16)
+    da_ref[...] = (grad * up * sig * (1.0 + pre * (1.0 - sig))).astype(jnp.bfloat16)
+    du_ref[...] = (grad * pre * sig).astype(jnp.bfloat16)
+
+
+def hidden_grads(expert_rows, grad_rows, w_gate, w_up, w_down):
+    rows, width = expert_rows.shape
+    units = w_gate.shape[2]
+    tile = 256 if units % 256 == 0 else units
+    shape = jax.ShapeDtypeStruct((rows, units), jnp.bfloat16)
+    part = pl.BlockSpec((rows, tile), lambda i: (0, i))
+    whole = pl.BlockSpec((rows, width), lambda i: (0, 0), pipeline_mode=pl.Buffered(1))
+    return pl.pallas_call(
+        hidden_kernel,
+        grid=(units // tile,),
+        out_shape=(shape, shape, shape),
+        in_specs=[
+            whole,
+            whole,
+            pl.BlockSpec((1, width, tile), lambda i: (0, 0, i)),
+            pl.BlockSpec((1, width, tile), lambda i: (0, 0, i)),
+            pl.BlockSpec((1, tile, width), lambda i: (0, i, 0)),
+        ],
+        out_specs=(part, part, part),
+        compiler_params=pltpu.CompilerParams(vmem_limit_bytes=44 * 1024 * 1024),
+        cost_estimate=pl.CostEstimate(
+            flops=6 * rows * width * units,
+            bytes_accessed=6 * width * units,
+            transcendentals=rows * units,
+        ),
+    )(expert_rows, grad_rows, w_gate, w_up, w_down)
+
+
 def slot_table(route_ids, experts, capacity):
     flat_ids = route_ids.reshape(-1)
     hits = (flat_ids[:, None] == jnp.arange(experts, dtype=jnp.int32)[None, :]).astype(jnp.int32)
@@ -271,10 +314,9 @@
     gate_w = w_gate[0]
     up_w = w_up[0]
     down_w = w_down[0]
-    pre_gate = jnp.dot(expert_rows, gate_w, preferred_element_type=jnp.float32)
-    pre_up = jnp.dot(expert_rows, up_w, preferred_element_type=jnp.float32)
-    sig_gate = jax.nn.sigmoid(pre_gate)
-    hidden = (pre_gate * sig_gate * pre_up).astype(jnp.bfloat16)
+    hidden, grad_pre_gate, grad_pre_up = hidden_grads(
+        expert_rows, grad_rows, w_gate, w_up, w_down
+    )
     summed_out = lax.psum_scatter(
         jnp.dot(hidden, down_w, preferred_element_type=jnp.float32).astype(jnp.bfloat16),
         "hidden",
@@ -286,11 +328,6 @@
     layer_out = jnp.dot(
         weighted, returned.reshape(-1, width).astype(jnp.float32), precision=lax.Precision.HIGHEST
     ).astype(jnp.bfloat16)
-    grad_hidden = jnp.dot(grad_rows, down_w.T, preferred_element_type=jnp.float32)
-    grad_pre_gate = (grad_hidden * pre_up * sig_gate * (1.0 + pre_gate * (1.0 - sig_gate))).astype(
-        jnp.bfloat16
-    )
-    grad_pre_up = (grad_hidden * pre_gate * sig_gate).astype(jnp.bfloat16)
     grad_down = jnp.dot(hidden.T, grad_rows, preferred_element_type=jnp.float32).astype(
         jnp.bfloat16
     )

time: 168 us -> 165 us (0.982)
  matrix products: 64.5 us -> 44.7 us
  Pallas kernels: 40.8 us -> 57.1 us
    dot_general x3 -> x0, matrix products: 19.7 us -> none  [the longest x1 9.76 us: on_device(): jnp.dot(grad_rows, down_w.T, preferred_element_type=jnp.float32)]
    pallas_call x0 -> x1, Pallas kernels: none -> 16.3 us  [hidden_grads(): pl.pallas_call(hidden_kernel, grid=(units // tile,), out_shape=(shape, sh...]
    unnamed x27 -> x25, local copies, waits for them, and re-layouts: 5.78 us -> 6.47 us
where the time goes in v2:
time: 165 us
  Pallas kernels  57.1 us (35%)
  matrix products  44.7 us (27%)
  waiting for transfers between devices  26.2 us (16%)
  between operations  14.4 us (9%)
  local copies, waits for them, and re-layouts  11.2 us (7%)
  starting transfers between devices  7.04 us (4%)
  other arithmetic  3.78 us (2%)
    pallas_call x1, Pallas kernels, gather_blocks(): pl.pallas_call(functools.partial(gather_kernel, experts, hidden), out_sha...  36.6 us
    reduce_scatter x1, waiting for transfers between devices, on_device(): lax.psum_scatter((first + jnp.dot(grad_pre_up, up_w.T, preferred_element_...  21.9 us
    pallas_call x1, Pallas kernels, hidden_grads(): pl.pallas_call(hidden_kernel, grid=(units // tile,), out_shape=(shape, sh...  16.3 us
    dot_general x1, matrix products, on_device(): first = jnp.dot(grad_pre_gate, gate_w.T, preferred_element_type=jnp.float32)  10.2 us
    dot_general x1, matrix products, on_device(): jnp.dot(grad_pre_up, up_w.T, preferred_element_type=jnp.float32)  8.82 us
    dot_general x1, matrix products, on_device(): jnp.dot(hidden.T, grad_rows, preferred_element_type=jnp.float32)  7.61 us
    dot_general x1, matrix products, on_device(): jnp.dot(expert_rows.T, grad_pre_up, preferred_element_type=jnp.float32)  6.6 us
    dot_general x1, matrix products, on_device(): jnp.dot(expert_rows.T, grad_pre_gate, preferred_element_type=jnp.float32)  6.6 us
  transfers between devices with their start and end apart: 4, of which 2 were waited for; matrix products, arithmetic and copies ran while one was open for 27% of the time, Pallas kernels for 0%

profile of v2, /device:TPU:0, one launch (start us, length us, event | category | flops | bytes accessed | tf_op | source)
XLA Modules:
  0.0 164.5 jit_solution(300135697328249691)
XLA Ops:
  7.3 0.7 convert_convert_fusion
  8.0 0.7 reduce-precision_convert_fusion.1
  8.7 0.1 copy.58
  8.9 1.0 pad_maximum_fusion.1
  9.9 0.1 reshape.281
  10.1 36.6 %shard_map.110 = bf16[32,48,1664]{2,1,0:T(8,128)(2,1)S(1)} custom-call(bf16[48,1664]{1,0:T(8,128)(2,1)S(1)} %reshape.282.blk_ref), custom_call_target="tpu_custom_call" | custom-call | tf_op jit(solution)/shard_map/pallas_call | solution.py:158
  46.8 2.3 %copy-done = bf16[32,48,1664]{2,1,0:T(8,128)(2,1)} copy-done((bf16[32,48,1664]{2,1,0:T(8,128)(2,1)}, bf16[32,48,1664]{2,1,0:T(8,128)(2,1)S(1)}, u32[]{:S(2)}) %copy-start) | copy-done | bytes 5111832
  49.1 0.2 slice_add_fusion
  49.2 0.1 copy.54
  49.4 0.1 copy.50
  49.5 0.1 copy.51
  49.7 0.1 multiply_reduce_fusion
  49.8 0.1 copy.55
  49.9 0.1 reshape.291.scale_ref
  50.0 0.1 copy.52
  50.1 0.1 convert_element_type.93
  50.3 0.1 broadcast_compare_fusion
  50.4 0.3 fusion.15
  50.7 0.1 broadcast_multiply_fusion.pick_ref
  50.9 2.4 %copy-done.1 = bf16[32,48,1664]{2,1,0:T(8,128)(2,1)S(1)} copy-done((bf16[32,48,1664]{2,1,0:T(8,128)(2,1)S(1)}, bf16[32,48,1664]{2,1,0:T(8,128)(2,1)}, u32[]{:S(2)}) %copy-start.1) | copy-done | bytes 5111832
  53.3 4.2 %shard_map.111 = (bf16[128,6144]{1,0:T(8,128)(2,1)S(1)}, bf16[128,6144]{1,0:T(8,128)(2,1)S(1)}) custom-call(bf16[2,4,128,768]{3,2,1,0:T(8,128)(2,1)S(1)} %broadcast_multiply_fusion.pick_ref, f32[128,1]{1,0:T(8,128)S(1)} %reshape.291.scale_ref, bf16[1536,1664]{1,0:T(8,128)(2,1)S(1)} %bitcast.49), custom_call_target="tpu_custom_call" | custom-call | tf_op jit(solution)/shard_map/pallas_call | solution.py:230
  57.5 16.3 %shard_map.112 = (bf16[128,1024]{1,0:T(8,128)(2,1)S(1)}, bf16[128,1024]{1,0:T(8,128)(2,1)S(1)}, bf16[128,1024]{1,0:T(8,128)(2,1)S(1)}) custom-call(bf16[128,6144]{1,0:T(8,128)(2,1)S(1)} %get-tuple-element.10.x_ref, bf16[128,6144]{1,0:T(8,128)(2,1)S(1)} %get-tuple-element.11.g_ref, bf16[1,6144,1024]{2,1,0:T(8,128)(2,1)} %gate_ref.1, ...), custom_call_target="tpu_custom_call" | custom-call | flops 4831838208 | bytes 37748736 | tf_op jit(solution)/shard_map/pallas_call | solution.py:269
  73.9 0.7 copy-done.2
  74.6 0.7 copy-done.5
  75.3 3.0 %fusion.12 = bf16[128,6144]{1,0:T(8,128)(2,1)} fusion(bf16[128,1024]{1,0:T(8,128)(2,1)S(1)} %get-tuple-element.12, bf16[1,1024,6144]{2,1,0:T(8,128)(2,1)S(1)} %bitcast.51), kind=kOutput, calls=%fused_computation.11 | convolution fusion | flops 1611399168 | bytes 14417920 | tf_op jit(solution)/shard_map/dot_general | solution.py:321
  78.3 0.2 reduce-scatter.5.cloned.1.call-start
  78.5 8.8 %fusion = f32[128,6144]{1,0:T(8,128)S(1)} fusion(bf16[128,1024]{1,0:T(8,128)(2,1)S(1)} %get-tuple-element.14, bf16[1,6144,1024]{2,1,0:T(8,128)(2,1)} %up_ref.1), kind=kOutput, calls=%fused_computation | convolution fusion | flops 1610612736 | bytes 15990784 | tf_op jit(solution)/shard_map/dot_general | solution.py:342
  87.4 10.2 %fusion.9 = bf16[128,6144]{1,0:T(8,128)(2,1)} fusion(f32[128,6144]{1,0:T(8,128)S(1)} %fusion, bf16[128,1024]{1,0:T(8,128)(2,1)S(1)} %copy-done.3, bf16[1,6144,1024]{2,1,0:T(8,128)(2,1)} %gate_ref.1), kind=kOutput, calls=%fused_computation.10 | convolution fusion | flops 1612185600 | bytes 17563648 | tf_op jit(solution)/shard_map/dot_general | solution.py:340
  97.6 0.1 copy.42
  97.7 0.1 eq.142
  97.7 0.1 fusion.21
  97.8 0.1 copy.44
  97.9 0.3 multiply_reduce_fusion.1
  98.2 0.2 select_reduce_fusion.1
  98.4 0.1 reduce_sum.67
  98.5 7.6 %convert_bitcast_fusion = bf16[1,1024,6144]{2,1,0:T(8,128)(2,1)} fusion(bf16[128,1024]{1,0:T(8,128)(2,1)} %copy-done.5, bf16[128,6144]{1,0:T(8,128)(2,1)S(1)} %get-tuple-element.11.g_ref), kind=kOutput, calls=%fused_computation.6 | convolution fusion | flops 1616904192 | bytes 14417920 | tf_op jit(solution)/shard_map/dot_general | solution.py:331
  106.1 6.6 %convert_bitcast_fusion.2 = bf16[1,6144,1024]{2,1,0:T(8,128)(2,1)} fusion(bf16[128,6144]{1,0:T(8,128)(2,1)S(1)} %get-tuple-element.10.x_ref, bf16[128,1024]{1,0:T(8,128)(2,1)S(1)} %copy-done.4), kind=kOutput, calls=%fused_computation.8 | convolution fusion | flops 1616904192 | bytes 14417920 | tf_op jit(solution)/shard_map/dot_general | solution.py:334
  112.7 6.6 %convert_bitcast_fusion.1 = bf16[1,6144,1024]{2,1,0:T(8,128)(2,1)} fusion(bf16[128,6144]{1,0:T(8,128)(2,1)S(1)} %get-tuple-element.10.x_ref, bf16[128,1024]{1,0:T(8,128)(2,1)S(1)} %get-tuple-element.14), kind=kOutput, calls=%fused_computation.7 | convolution fusion | flops 1616904192 | bytes 14417920 | tf_op jit(solution)/shard_map/dot_general | solution.py:337
  119.3 1.7 %reshape.285 = bf16[4,4,6144]{2,1,0:T(4,128)(2,1)} reshape(bf16[16,6144]{1,0:T(8,128)(2,1)} %reduce-scatter.3.cloned.1.call-done) | data formatting | bytes 393216 | tf_op jit(solution)/shard_map/reshape | solution.py:326
  121.0 3.4 %all-to-all-start = ((bf16[4,4,6144]{2,1,0:T(4,128)(2,1)}), bf16[4,4,6144]{2,1,0:T(4,128)(2,1)S(1)}, u32[]{:S(2)}, u32[]{:S(2)}) async-start(bf16[4,4,6144]{2,1,0:T(4,128)(2,1)} %reshape.285), calls=%async_computation.1 | async-start | bytes 393216 | tf_op jit(solution)/shard_map/all_to_all | solution.py:327
  124.4 0.1 copy.46
  124.5 0.1 convert_reduce_fusion.1
  124.6 21.9 %reduce-scatter.5.cloned.1.call-done = bf16[16,6144]{1,0:T(8,128)(2,1)} async-done(((bf16[128,6144]{1,0:T(8,128)(2,1)}), bf16[16,6144]{1,0:T(8,128)(2,1)}) %reduce-scatter.5.cloned.1.call-update) | async-done | bytes 196624 | tf_op jit(solution)/shard_map/reduce_scatter | solution.py:341
  146.5 1.7 %reshape.287 = bf16[4,4,6144]{2,1,0:T(4,128)(2,1)} reshape(bf16[16,6144]{1,0:T(8,128)(2,1)} %reduce-scatter.5.cloned.1.call-done) | data formatting | bytes 393216 | tf_op jit(solution)/shard_map/reshape | solution.py:349
  148.2 3.4 %all-to-all-start.1 = ((bf16[4,4,6144]{2,1,0:T(4,128)(2,1)}), bf16[4,4,6144]{2,1,0:T(4,128)(2,1)S(1)}, u32[]{:S(2)}, u32[]{:S(2)}) async-start(bf16[4,4,6144]{2,1,0:T(4,128)(2,1)} %reshape.287), calls=%async_computation.3 | async-start | bytes 393216 | tf_op jit(solution)/shard_map/all_to_all | solution.py:350
  151.6 0.9 convolution_convert_fusion.1
  152.5 4.3 %all-to-all-done.1 = bf16[4,4,6144]{2,1,0:T(4,128)(2,1)S(1)} async-done(((bf16[4,4,6144]{2,1,0:T(4,128)(2,1)}), bf16[4,4,6144]{2,1,0:T(4,128)(2,1)S(1)}, u32[]{:S(2)}, u32[]{:S(2)}) %all-to-all-start.1) | async-done | bytes 196640 | tf_op jit(solution)/shard_map/all_to_all | solution.py:350
  156.8 0.9 convolution_convert_fusion
  (50 shorter events, 0.7 us)
Async XLA Ops:
  7.2 112.1 %reduce-scatter.3.cloned.1.call-start = ((), (), s32[]{:S(2)}) async-start(), calls=%async_computation.4 | async-start | bytes 1769472 | tf_op jit(solution)/shard_map/reduce_scatter | solution.py:320
  46.8 2.3 %copy-start = (bf16[32,48,1664]{2,1,0:T(8,128)(2,1)}, bf16[32,48,1664]{2,1,0:T(8,128)(2,1)S(1)}, u32[]{:S(2)}) copy-start(bf16[32,48,1664]{2,1,0:T(8,128)(2,1)S(1)} %shard_map.110) | copy-start | bytes 15335428
  50.9 2.5 %copy-start.1 = (bf16[32,48,1664]{2,1,0:T(8,128)(2,1)S(1)}, bf16[32,48,1664]{2,1,0:T(8,128)(2,1)}, u32[]{:S(2)}) copy-start(bf16[32,48,1664]{2,1,0:T(8,128)(2,1)} %copy-done) | copy-start | bytes 15335428
  53.3 22.0 %slice-start = ((s8[12582912]{0:T(1024)(128)(4,1)}), s8[4194304]{0:T(1024)(128)(4,1)S(1)}, s32[]{:S(2)}) async-start(s8[12582912]{0:T(1024)(128)(4,1)} %bitcast.50), calls=%async_computation.6 | async-start | bytes 8388608
  57.5 17.8 %slice-start.1 = ((s8[12582912]{0:T(1024)(128)(4,1)}), s8[4194304]{0:T(1024)(128)(4,1)S(1)}, s32[]{:S(2)}) async-start(s8[12582912]{0:T(1024)(128)(4,1)} %bitcast.50), calls=%async_computation.7 | async-start | bytes 8388608
  57.5 17.8 %slice-start.2 = ((s8[12582912]{0:T(1024)(128)(4,1)}), s8[4194304]{0:T(1024)(128)(4,1)S(1)}, s32[]{:S(2)}) async-start(s8[12582912]{0:T(1024)(128)(4,1)} %bitcast.50), calls=%async_computation.8 | async-start | bytes 8388608
  73.9 0.7 copy-start.2
  74.6 0.7 copy-start.5
  78.3 68.2 %reduce-scatter.5.cloned.1.call-start = ((), (), s32[]{:S(2)}) async-start(), calls=%async_computation.5 | async-start | bytes 1769472 | tf_op jit(solution)/shard_map/reduce_scatter | solution.py:341
  78.5 8.8 %copy-start.3 = (bf16[128,1024]{1,0:T(8,128)(2,1)S(1)}, bf16[128,1024]{1,0:T(8,128)(2,1)}, u32[]{:S(2)}) copy-start(bf16[128,1024]{1,0:T(8,128)(2,1)} %copy-done.2) | copy-start | bytes 786436
  87.4 10.2 %copy-start.7 = (s32[6,2]{0,1:T(2,128)S(1)}, s32[6,2]{0,1:T(2,128)}, u32[]{:S(2)}) copy-start(s32[6,2]{0,1:T(2,128)} %param.8) | copy-start | bytes 148
  98.5 7.6 %copy-start.4 = (bf16[128,1024]{1,0:T(8,128)(2,1)S(1)}, bf16[128,1024]{1,0:T(8,128)(2,1)}, u32[]{:S(2)}) copy-start(bf16[128,1024]{1,0:T(8,128)(2,1)} %copy-done.2) | copy-start | bytes 786436
  112.7 11.7 %copy-start.6 = (f32[6,2]{0,1:T(2,128)S(1)}, f32[6,2]{0,1:T(2,128)}, u32[]{:S(2)}) copy-start(f32[6,2]{0,1:T(2,128)} %param.9) | copy-start | bytes 148
  121.0 27.2 %all-to-all-start = ((bf16[4,4,6144]{2,1,0:T(4,128)(2,1)}), bf16[4,4,6144]{2,1,0:T(4,128)(2,1)S(1)}, u32[]{:S(2)}, u32[]{:S(2)}) async-start(bf16[4,4,6144]{2,1,0:T(4,128)(2,1)} %reshape.285), calls=%async_computation.1 | async-start | bytes 393216 | tf_op jit(solution)/shard_map/all_to_all | solution.py:327
  148.2 8.6 %all-to-all-start.1 = ((bf16[4,4,6144]{2,1,0:T(4,128)(2,1)}), bf16[4,4,6144]{2,1,0:T(4,128)(2,1)S(1)}, u32[]{:S(2)}, u32[]{:S(2)}) async-start(bf16[4,4,6144]{2,1,0:T(4,128)(2,1)} %reshape.287), calls=%async_computation.3 | async-start | bytes 393216 | tf_op jit(solution)/shard_map/all_to_all | solution.py:350
Sparse Core Ops, SparseCore 0:
  78.4 33.4 reduce-scatter.2
  114.2 32.2 reduce-scatter.4
